TPU v7x, 32 devices: a whole 2x2x4 slice. The times are simulated.
32 devices in a mesh: tile: 4 (over y, x), thick: 8 (over z, core).
Axes of the slice: x: 2, y: 2, z: 4, core: 2. Of those that a mesh axis runs over, the one named last changes fastest.
Arguments:
- concentration: float32 [2, 64, 512, 256], P(None, 'tile', 'thick'), may hold values from 0 to 1
- polymer: float32 [64, 512, 256], P('tile', 'thick'), may hold values from 0.5 to 2
- plates: int32 [256, 6], P('tile'), may hold values from 0 to 511, as said below
Outputs:
- final_conc: float32 [2, 64, 512, 256], P(None, 'tile', 'thick')
Inputs may be any that keep to these rules, and one draw needn't show every extreme that they name: `plates`: each row is one platelet; the x length is 1 to 16 and the x range wraps modulo 64; the y and z ranges lie inside the grid. Of the rows held by one device of tile, at most 32 cover cells of any one tile's 16 x positions, and in every draw some tile is covered by exactly 32 rows of every device.
All inputs are finite; a program needn't handle non-finite values.
Results may differ from a plain program's by a relative error of at most 0.0003.
Values sent between devices are 32-bit elements; how exact they have to be, the bound alone decides.
A program may use at most 128 MiB of HBM per device.

v0:
```python
import functools

import jax
import jax.numpy as jnp
from jax import lax
from jax.experimental import pallas as pl
from jax.experimental.pallas import tpu as pltpu
from jax.sharding import PartitionSpec as P

STEPS = 2
BLOCKING = 9.0
PLANE_RATE = 0.11
LINE_RATE = 1000.0
RATIOS = (1.0, 0.6)
F32 = jnp.float32
ROWS = 8
LANES = 128


def kernel(tiles, layers, conc, poly, rec, out, recg, zs, hz, hp, base, ca, cb, rhs,
           inv, low, fac, spike_p, spike_q, val, coef_out, coef_in, red, ends_out, ends_in,
           reply, sides, rec_s, rec_r, zh_s, zh_r, ph_s, ph_r, ch_s, ch_r, co_s, co_r,
           en_s, en_r, re_s, re_r):
    species, rows_x, rows_z, width_y = conc.shape
    halves = width_y // LANES
    groups = rows_x // ROWS
    per = groups * halves
    chunks = species * per
    tile = lax.axis_index("tile")
    layer = lax.axis_index("thick")
    width_x = tiles * rows_x
    every = layers == chunks

    def tile_at(d):
        return lax.rem(tile + d + tiles, tiles)

    def layer_at(d):
        return lax.rem(layer + d + layers, layers)

    def when(cond, fn):
        if every:
            fn()
        else:
            pl.when(cond)(fn)

    def remote(src, dst, send, recv, where):
        return pltpu.make_async_remote_copy(
            src_ref=src, dst_ref=dst, send_sem=send, recv_sem=recv,
            device_id=where, device_id_type=pl.DeviceIdType.MESH)

    barrier = pltpu.get_barrier_semaphore()
    for d in range(1, tiles):
        pl.semaphore_signal(barrier, inc=1, device_id=(tile_at(d), layer),
                            device_id_type=pl.DeviceIdType.MESH)
    for d in range(1, layers):
        pl.semaphore_signal(barrier, inc=1, device_id=(tile, layer_at(d)),
                            device_id_type=pl.DeviceIdType.MESH)

    def copy_plane(x):
        dst = pl.ds(pl.multiple_of((x + 1) * rows_z, rows_z), rows_z)
        for s in range(species):
            for j in range(halves):
                ca[s, j, dst, :] = conc[s, x, :, j * LANES:(j + 1) * LANES]

    copy_plane(0)
    copy_plane(rows_x - 1)
    zs[0] = poly[:, rows_z - 1, :]
    zs[1] = poly[:, 0, :]
    recg[0] = rec[...]
    pl.semaphore_wait(barrier, tiles - 1 + layers - 1)

    pending = []
    rec_copies = [
        remote(rec, recg.at[d], rec_s.at[d], rec_r.at[d], (tile_at(d), layer))
        for d in range(1, tiles)
    ]
    zh_copies = [
        remote(zs.at[0], hz.at[0], zh_s.at[0], zh_r.at[0], (tile, layer_at(1))),
        remote(zs.at[1], hz.at[1], zh_s.at[1], zh_r.at[1], (tile, layer_at(-1))),
    ]
    ph_copies = [
        remote(poly.at[rows_x - 1], hp.at[0], ph_s.at[0], ph_r.at[0], (tile_at(1), layer)),
        remote(poly.at[0], hp.at[1], ph_s.at[1], ph_r.at[1], (tile_at(-1), layer)),
    ]

    def plane_copies(c, step):
        last = pl.ds(rows_x * rows_z, rows_z)
        first = pl.ds(rows_z, rows_z)
        over = pl.ds((rows_x + 1) * rows_z, rows_z)
        under = pl.ds(0, rows_z)
        return [
            remote(c.at[:, :, last, :], c.at[:, :, under, :], ch_s.at[step, 0],
                   ch_r.at[step, 0], (tile_at(1), layer)),
            remote(c.at[:, :, first, :], c.at[:, :, over, :], ch_s.at[step, 1],
                   ch_r.at[step, 1], (tile_at(-1), layer)),
        ]

    ch_copies = plane_copies(ca, 0)
    for copy in rec_copies + zh_copies + ph_copies + ch_copies:
        copy.start()
    pending += rec_copies + zh_copies + ph_copies + ch_copies

    @pl.loop(1, rows_x - 1)
    def _(x):
        copy_plane(x)

    for copy in rec_copies:
        copy.wait_recv()
    table = jnp.concatenate([recg[d] for d in range(tiles)], axis=1)
    total = table.shape[1]
    start_x, len_x = table[0:1], table[1:2]
    start_y, len_y = table[2:3], table[3:4]
    start_z, len_z = table[4:5], table[5:6]

    def wrap(value):
        if width_x & (width_x - 1) == 0:
            return value & (width_x - 1)
        return jnp.mod(value, width_x)

    def inside(pos, start, length):
        return jnp.where((pos >= start) & (pos < start + length), 1.0, 0.0)

    pos_y = lax.broadcasted_iota(jnp.int32, (width_y, total), 0)
    in_y = inside(pos_y, start_y, len_y).astype(jnp.bfloat16)
    pos_z = layer * rows_z + lax.broadcasted_iota(jnp.int32, (rows_z, total), 0)
    in_z = inside(pos_z, start_z, len_z)

    def counted(mask):
        return lax.dot_general(mask.astype(jnp.bfloat16), in_y, (((1,), (1,)), ((), ())),
                               preferred_element_type=F32)

    def put_base(x, polymer):
        in_x = jnp.where(wrap(tile * rows_x + x - start_x) < len_x, 1.0, 0.0)
        values = polymer / (1.0 + BLOCKING * counted(in_z * in_x))
        dst = pl.ds(pl.multiple_of((x + 1) * rows_z, rows_z), rows_z)
        for j in range(halves):
            base[j, dst, :] = values[:, j * LANES:(j + 1) * LANES]

    @pl.loop(0, rows_x)
    def _(x):
        put_base(x, poly[x])

    for copy in zh_copies:
        copy.wait_recv()
    pos_x = tile * rows_x + lax.broadcasted_iota(jnp.int32, (rows_x, total), 0)
    in_x_all = jnp.where(wrap(pos_x - start_x) < len_x, 1.0, 0.0)

    def z_halo(side, z):
        mask = in_x_all * inside(z, start_z, len_z)
        values = hz[side] / (1.0 + BLOCKING * counted(mask))
        return jnp.stack([values[g * ROWS:(g + 1) * ROWS, j * LANES:(j + 1) * LANES]
                          for g in range(groups) for j in range(halves)])

    def base_row(z):
        return jnp.stack([
            base[j, pl.ds((1 + g * ROWS) * rows_z + z, ROWS, stride=rows_z), :]
            for g in range(groups) for j in range(halves)])

    first_base = base_row(0)
    last_base = base_row(rows_z - 1)
    under_base = jnp.where(layer == 0, first_base, z_halo(0, layer * rows_z - 1))
    over_base = jnp.where(layer == layers - 1, last_base, z_halo(1, (layer + 1) * rows_z))

    def factor_row(z, carry, above):
        below, here, prior_f, prior_p = carry
        lower = 0.5 * (below + here)
        upper = 0.5 * (here + above)
        lw = jnp.concatenate([r * lower for r in RATIOS], axis=0)
        up = jnp.concatenate([r * upper for r in RATIOS], axis=0)
        l = -LINE_RATE * lw
        pivot = (1.0 + LINE_RATE * (lw + up)) - l * prior_f
        i = 1.0 / pivot
        f = (-LINE_RATE * up) * i
        li = l * i
        p = -(li * prior_p)
        inv[z] = i
        low[z] = li
        fac[z] = f
        spike_p[z] = p
        return (here, above, f, p)

    shape = (chunks, ROWS, LANES)
    carry = (under_base, first_base, jnp.zeros(shape, F32), jnp.ones(shape, F32))
    carry = lax.fori_loop(0, rows_z - 1, lambda z, c: factor_row(z, c, base_row(z + 1)), carry)
    factor_row(rows_z - 1, carry, over_base)

    unroll = 4

    def spike_rows(n, carry):
        p, q = carry
        for m in range(unroll):
            z = rows_z - 1 - (n * unroll + m)
            f = fac[z]
            p = spike_p[z] - f * p
            q = -(f * q)
            spike_p[z] = p
            spike_q[z] = q
        return p, q

    lax.fori_loop(0, rows_z // unroll, spike_rows, (jnp.zeros(shape, F32), jnp.ones(shape, F32)))

    for member, value in enumerate((spike_p[0], spike_q[0], spike_p[rows_z - 1],
                                    spike_q[rows_z - 1])):
        for c in range(chunks):
            coef_out[c, member] = value[c]

    def to_owner(src, dst, send, recv, d):
        owner = layer_at(d)
        return owner, remote(src.at[owner if every else lax.rem(owner, chunks)], dst.at[layer],
                             send, recv, (tile, owner))

    def send_owned(src, dst, send, recv):
        for d in range(1, layers):
            owner, copy = to_owner(src, dst, send(d), recv(d), d)
            when(owner < chunks, copy.start)

        def keep():
            dst[layer] = src[layer if every else lax.rem(layer, chunks)]

        when(layer < chunks, keep)

    def wait_owned(src, dst, send, recv):
        for d in range(1, layers):
            copy = to_owner(src, dst, send(d), recv(d), d)[1]
            when(layer < chunks, copy.wait_recv)

    def drain_owned(src, dst, send, recv):
        for d in range(1, layers):
            owner, copy = to_owner(src, dst, send(d), recv(d), d)
            when(owner < chunks, copy.wait_send)

    coef_args = (coef_out, coef_in, lambda d: co_s.at[d], lambda d: co_r.at[d])
    send_owned(*coef_args)

    for copy in ph_copies:
        copy.wait_recv()
    put_base(-1, hp[0])
    put_base(rows_x, hp[1])

    lane = lax.broadcasted_iota(jnp.int32, (16, LANES), 1)

    def next_y(parts):
        turned = [pltpu.roll(v, LANES - 1, 1) for v in parts]
        return [jnp.where(lane == LANES - 1, turned[(j + 1) % halves], turned[j])
                for j in range(halves)]

    def prior_y(parts):
        turned = [pltpu.roll(v, 1, 1) for v in parts]
        return [jnp.where(lane == 0, turned[j - 1], turned[j]) for j in range(halves)]

    def plane_x(c, x):
        for z in range(0, rows_z, 16):
            under = pl.ds(pl.multiple_of(x * rows_z, rows_z) + z, 16)
            here = pl.ds(pl.multiple_of((x + 1) * rows_z, rows_z) + z, 16)
            over = pl.ds(pl.multiple_of((x + 2) * rows_z, rows_z) + z, 16)
            b = [base[j, here, :] for j in range(halves)]
            b_next = next_y(b)
            face_xm = [0.5 * (base[j, under, :] + b[j]) for j in range(halves)]
            face_xp = [0.5 * (b[j] + base[j, over, :]) for j in range(halves)]
            face_y = [0.5 * (b[j] + b_next[j]) for j in range(halves)]
            for s in range(species):
                v = [c[s, j, here, :] for j in range(halves)]
                v_next = next_y(v)
                flux = [face_y[j] * (v_next[j] - v[j]) for j in range(halves)]
                back = prior_y(flux)
                for j in range(halves):
                    along = (face_xp[j] * (c[s, j, over, :] - v[j])
                             - face_xm[j] * (v[j] - c[s, j, under, :]))
                    rhs[s, j, under, :] = v[j] + (PLANE_RATE * RATIOS[s]) * (
                        along + (flux[j] - back[j]))

    def strided(ref, z, pad):
        return jnp.stack([
            ref[s, j, pl.ds((pad + g * ROWS) * rows_z + z, ROWS, stride=rows_z), :]
            for s in range(species) for g in range(groups) for j in range(halves)])

    def put_strided(ref, z, pad, value):
        n = 0
        for s in range(species):
            for g in range(groups):
                for j in range(halves):
                    ref[s, j, pl.ds((pad + g * ROWS) * rows_z + z, ROWS, stride=rows_z), :] = value[n]
                    n += 1

    def forward_rows(n, state):
        for m in range(unroll):
            z = n * unroll + m
            state = strided(rhs, z, 0) * inv[z] - low[z] * state
            val[z] = state
        return state

    def backward_rows(n, v):
        for m in range(unroll):
            z = rows_z - 1 - (n * unroll + m)
            v = val[z] - fac[z] * v
            val[z] = v
        return v

    def reduce_matrix():
        wait_owned(*coef_args)
        b = jnp.zeros((ROWS, LANES), F32)
        for k in range(layers):
            red[k, 2] = b
            d = 1.0 / (1.0 - coef_in[k, 0] * b)
            g = coef_in[k, 2] * b * d
            b = coef_in[k, 3] + g * coef_in[k, 1]
            red[k, 0] = d
            red[k, 1] = g

    def reduce_solve(step):
        top = jnp.where(layer < per, 1.0, 0.0)
        a = jnp.full((ROWS, LANES), top, F32)
        prior = []
        heads = []
        for k in range(layers):
            prior.append(a)
            head = ends_in[step, k, 0] + coef_in[k, 0] * a
            heads.append(head)
            a = ends_in[step, k, 1] + coef_in[k, 2] * a + red[k, 1] * head
        f = jnp.full((ROWS, LANES), 1.0 - top, F32)
        for k in range(layers - 1, -1, -1):
            reply[step, k, 1] = f
            f = red[k, 0] * (heads[k] + coef_in[k, 1] * f)
            reply[step, k, 0] = prior[k] + red[k, 2] * f

    def reply_copy(step, d):
        peer = layer_at(d)
        mine = layer if every else lax.rem(layer, chunks)
        return remote(reply.at[step, peer], sides.at[step, mine], re_s.at[step, d],
                      re_r.at[step, d], (tile, peer))

    for step in range(STEPS):
        c_in = ca if step == 0 else cb
        for copy in ch_copies:
            copy.wait_recv()

        @pl.loop(0, rows_x)
        def _(x, c_in=c_in):
            plane_x(c_in, x)

        lax.fori_loop(0, rows_z // unroll, forward_rows, jnp.zeros(shape, F32))
        first = lax.fori_loop(0, rows_z // unroll, backward_rows, jnp.zeros(shape, F32))
        last = val[rows_z - 1]
        for c in range(chunks):
            ends_out[step, c, 0] = first[c]
            ends_out[step, c, 1] = last[c]
        ends_args = (ends_out.at[step], ends_in.at[step],
                     lambda d, step=step: en_s.at[step, d], lambda d, step=step: en_r.at[step, d])
        send_owned(*ends_args)
        if step == 0:
            when(layer < chunks, reduce_matrix)
        wait_owned(*ends_args)

        def answer(step=step):
            reduce_solve(step)
            for d in range(1, layers):
                reply_copy(step, d).start()
            sides[step, layer if every else lax.rem(layer, chunks)] = reply[step, layer]

        when(layer < chunks, answer)
        for d in range(1, layers):
            when(layer_at(-d) < chunks, reply_copy(step, d).wait_recv)
        before = sides[step, :, 0]
        after = sides[step, :, 1]

        def finish_rows(n, carry):
            for m in range(unroll):
                z = n * unroll + m
                put_strided(cb if step + 1 < STEPS else ca, z, 1,
                            val[z] + spike_p[z] * before + spike_q[z] * after)
            return carry

        lax.fori_loop(0, rows_z // unroll, finish_rows, 0)
        if step + 1 < STEPS:
            ch_copies = plane_copies(cb, step + 1)
            for copy in ch_copies:
                copy.start()
            pending += ch_copies
        if step == 0:
            for copy in pending:
                if not any(copy is other for other in ch_copies):
                    copy.wait_send()
            pending = list(ch_copies)
            drain_owned(*coef_args)
        drain_owned(*ends_args)
        for d in range(1, layers):
            when(layer < chunks, reply_copy(step, d).wait_send)

    @pl.loop(0, rows_x)
    def _(x):
        src = pl.ds(pl.multiple_of((x + 1) * rows_z, rows_z), rows_z)
        for s in range(species):
            for j in range(halves):
                out[s, x, :, j * LANES:(j + 1) * LANES] = ca[s, j, src, :]

    for copy in pending:
        copy.wait_send()


def on_device(concentration, polymer, plates):
    species, rows_x, rows_z, width_y = concentration.shape
    tiles = lax.axis_size("tile")
    layers = lax.axis_size("thick")
    halves = width_y // LANES
    chunks = species * (rows_x // ROWS) * halves
    count = plates.shape[0]
    records = jnp.pad(plates.T, ((0, 8 - plates.shape[1]), (0, -count % LANES)))
    line = pltpu.VMEM((rows_z, chunks, ROWS, LANES), F32)
    dma = pltpu.SemaphoreType.DMA
    extended = (halves, (rows_x + 2) * rows_z, LANES)
    scratch = [
        pltpu.VMEM((tiles,) + records.shape, jnp.int32),
        pltpu.VMEM((2, rows_x, width_y), F32),
        pltpu.VMEM((2, rows_x, width_y), F32),
        pltpu.VMEM((2, rows_z, width_y), F32),
        pltpu.VMEM(extended, F32),
        pltpu.VMEM((species,) + extended, F32),
        pltpu.VMEM((species,) + extended, F32),
        pltpu.VMEM((species, halves, rows_x * rows_z, LANES), F32),
        line, line, line, line, line, line,
        pltpu.VMEM((chunks, 4, ROWS, LANES), F32),
        pltpu.VMEM((layers, 4, ROWS, LANES), F32),
        pltpu.VMEM((layers, 3, ROWS, LANES), F32),
        pltpu.VMEM((STEPS, chunks, 2, ROWS, LANES), F32),
        pltpu.VMEM((STEPS, layers, 2, ROWS, LANES), F32),
        pltpu.VMEM((STEPS, layers, 2, ROWS, LANES), F32),
        pltpu.VMEM((STEPS, chunks, 2, ROWS, LANES), F32),
        dma((tiles,)), dma((tiles,)), dma((2,)), dma((2,)), dma((2,)), dma((2,)),
        dma((STEPS, 2)), dma((STEPS, 2)), dma((layers,)), dma((layers,)),
        dma((STEPS, layers)), dma((STEPS, layers)), dma((STEPS, layers)), dma((STEPS, layers)),
    ]
    vmem = pl.BlockSpec(memory_space=pltpu.VMEM)
    return pl.pallas_call(
        functools.partial(kernel, tiles, layers),
        out_shape=jax.ShapeDtypeStruct(concentration.shape, F32),
        in_specs=[vmem, vmem, vmem],
        out_specs=vmem,
        scratch_shapes=scratch,
        compiler_params=pltpu.CompilerParams(
            collective_id=0, has_side_effects=True, vmem_limit_bytes=48 * 2**20),
    )(concentration, polymer, records)


def solution(mesh):
    return jax.shard_map(
        on_device,
        mesh=mesh,
        in_specs=(P(None, "tile", "thick", None), P("tile", "thick", None), P("tile", None)),
        out_specs=P(None, "tile", "thick", None),
        check_vma=False,
    )
```

profile of v0, /device:TPU:0, one launch (start us, length us, event | category | flops | bytes accessed | tf_op | source)
XLA Modules:
  0.0 60.7 jit_solution(3826210872014073515)
XLA Ops:
  0.0 0.7 %pad.4.rec = s32[8,128]{1,0:T(8,128)S(1)} pad(s32[6,64]{1,0:T(8,128)} %bitcast.1, s32[]{:T(128)} %constant.0.clone.1), padding=0_2x0_64 | pad | bytes 5636 | tf_op jit(solution)/shard_map/jit(_pad)/pad | solution.py:407
  0.7 0.0 copy-start
  0.7 1.6 %copy-done = f32[2,16,64,256]{3,2,1,0:T(8,128)S(1)} copy-done((f32[2,16,64,256]{3,2,1,0:T(8,128)S(1)}, f32[2,16,64,256]{3,2,1,0:T(8,128)}, u32[]{:S(2)}) %copy-start) | copy-done | bytes 2097176
  2.3 0.0 copy-start.1
  2.3 1.2 %copy-done.1 = f32[16,64,256]{2,1,0:T(8,128)S(1)} copy-done((f32[16,64,256]{2,1,0:T(8,128)S(1)}, f32[16,64,256]{2,1,0:T(8,128)}, u32[]{:S(2)}) %copy-start.1) | copy-done | bytes 1048600
  3.5 55.9 %shard_map.37 = f32[2,16,64,256]{3,2,1,0:T(8,128)S(1)} custom-call(f32[2,16,64,256]{3,2,1,0:T(8,128)S(1)} %copy-done, f32[16,64,256]{2,1,0:T(8,128)S(1)} %copy-done.1, s32[8,128]{1,0:T(8,128)S(1)} %pad.4.rec), custom_call_target="tpu_custom_call" | custom-call | tf_op jit(solution)/shard_map/pallas_call | solution.py:433
  59.4 1.3 %copy.5 = f32[2,16,64,256]{3,2,1,0:T(8,128)} copy(f32[2,16,64,256]{3,2,1,0:T(8,128)S(1)} %shard_map.37) | data formatting | bytes 4194304
Async XLA Ops:
  0.7 1.6 %copy-start = (f32[2,16,64,256]{3,2,1,0:T(8,128)S(1)}, f32[2,16,64,256]{3,2,1,0:T(8,128)}, u32[]{:S(2)}) copy-start(f32[2,16,64,256]{3,2,1,0:T(8,128)} %conc.1) | copy-start | bytes 6291460
  2.3 1.2 %copy-start.1 = (f32[16,64,256]{2,1,0:T(8,128)S(1)}, f32[16,64,256]{2,1,0:T(8,128)}, u32[]{:S(2)}) copy-start(f32[16,64,256]{2,1,0:T(8,128)} %poly.1) | copy-start | bytes 3145732
where the time goes:
time: 60.9 us; the launch traced here: 60.7 us
  Pallas kernels  55.9 us (92%)
  local copies, waits for them, and re-layouts  4.83 us (8%)
    pallas_call x1, Pallas kernels, on_device(): pl.pallas_call(functools.partial(kernel, tiles, layers), out_shape=jax.Sh...  55.9 us
    unnamed x5, local copies, waits for them, and re-layouts  4.14 us

commit v1 on v0

--- a/solution.py
+++ b/solution.py
@@ -15,12 +15,13 @@
 F32 = jnp.float32
 ROWS = 8
 LANES = 128
-
-
-def kernel(tiles, layers, conc, poly, rec, out, recg, zs, hz, hp, base, ca, cb, rhs,
+PAD = 8
+
+
+def kernel(tiles, layers, conc, poly_in, rec, out, mine, recg, poly, zs, hz, hp, base, ca, cb, rhs,
            inv, low, fac, spike_p, spike_q, val, coef_out, coef_in, red, ends_out, ends_in,
            reply, sides, rec_s, rec_r, zh_s, zh_r, ph_s, ph_r, ch_s, ch_r, co_s, co_r,
-           en_s, en_r, re_s, re_r):
+           en_s, en_r, re_s, re_r, in_c, in_p):
     species, rows_x, rows_z, width_y = conc.shape
     halves = width_y // LANES
     groups = rows_x // ROWS
@@ -29,6 +30,7 @@
     tile = lax.axis_index("tile")
     layer = lax.axis_index("thick")
     width_x = tiles * rows_x
+    pitch = rows_z + PAD
     every = layers == chunks
 
     def tile_at(d):
@@ -56,22 +58,25 @@
         pl.semaphore_signal(barrier, inc=1, device_id=(tile, layer_at(d)),
                             device_id_type=pl.DeviceIdType.MESH)
 
-    def copy_plane(x):
-        dst = pl.ds(pl.multiple_of((x + 1) * rows_z, rows_z), rows_z)
+    poly_copy = pltpu.make_async_copy(poly_in, poly, in_p)
+    poly_copy.start()
+
+    @pl.loop(0, rows_x)
+    def _(x):
+        dst = pl.ds(pl.multiple_of((x + 1) * pitch, 8), rows_z)
         for s in range(species):
             for j in range(halves):
-                ca[s, j, dst, :] = conc[s, x, :, j * LANES:(j + 1) * LANES]
-
-    copy_plane(0)
-    copy_plane(rows_x - 1)
-    zs[0] = poly[:, rows_z - 1, :]
-    zs[1] = poly[:, 0, :]
-    recg[0] = rec[...]
+                pltpu.make_async_copy(conc.at[s, x, :, pl.ds(j * LANES, LANES)],
+                                      ca.at[s, j, dst, :], in_c).start()
+
+    mine[...] = jnp.zeros_like(mine)
+    mine[0:rec.shape[0], 0:rec.shape[1]] = rec[...]
+    recg[0] = mine[...]
     pl.semaphore_wait(barrier, tiles - 1 + layers - 1)
 
     pending = []
     rec_copies = [
-        remote(rec, recg.at[d], rec_s.at[d], rec_r.at[d], (tile_at(d), layer))
+        remote(mine, recg.at[d], rec_s.at[d], rec_r.at[d], (tile_at(d), layer))
         for d in range(1, tiles)
     ]
     zh_copies = [
@@ -79,34 +84,44 @@
         remote(zs.at[1], hz.at[1], zh_s.at[1], zh_r.at[1], (tile, layer_at(-1))),
     ]
     ph_copies = [
-        remote(poly.at[rows_x - 1], hp.at[0], ph_s.at[0], ph_r.at[0], (tile_at(1), layer)),
-        remote(poly.at[0], hp.at[1], ph_s.at[1], ph_r.at[1], (tile_at(-1), layer)),
+        remote(poly_in.at[rows_x - 1], hp.at[0], ph_s.at[0], ph_r.at[0], (tile_at(1), layer)),
+        remote(poly_in.at[0], hp.at[1], ph_s.at[1], ph_r.at[1], (tile_at(-1), layer)),
     ]
 
-    def plane_copies(c, step):
-        last = pl.ds(rows_x * rows_z, rows_z)
-        first = pl.ds(rows_z, rows_z)
-        over = pl.ds((rows_x + 1) * rows_z, rows_z)
-        under = pl.ds(0, rows_z)
+    def plane_copies(c, step, part):
+        span = rows_z // 2
+        low_row = part * span
+        last = pl.ds(rows_x * pitch + low_row, span)
+        first = pl.ds(pitch + low_row, span)
+        over = pl.ds((rows_x + 1) * pitch + low_row, span)
+        under = pl.ds(low_row, span)
         return [
-            remote(c.at[:, :, last, :], c.at[:, :, under, :], ch_s.at[step, 0],
-                   ch_r.at[step, 0], (tile_at(1), layer)),
-            remote(c.at[:, :, first, :], c.at[:, :, over, :], ch_s.at[step, 1],
-                   ch_r.at[step, 1], (tile_at(-1), layer)),
+            remote(c.at[:, :, last, :], c.at[:, :, under, :], ch_s.at[step, part, 0],
+                   ch_r.at[step, part, 0], (tile_at(1), layer)),
+            remote(c.at[:, :, first, :], c.at[:, :, over, :], ch_s.at[step, part, 1],
+                   ch_r.at[step, part, 1], (tile_at(-1), layer)),
         ]
 
-    ch_copies = plane_copies(ca, 0)
-    for copy in rec_copies + zh_copies + ph_copies + ch_copies:
+    for copy in rec_copies:
+        copy.start()
+    poly_copy.wait()
+    zs[0] = poly[:, rows_z - 1, :]
+    zs[1] = poly[:, 0, :]
+    for copy in zh_copies + ph_copies:
+        copy.start()
+    pltpu.make_async_copy(conc, out, in_c).wait()
+    ch_copies = plane_copies(ca, 0, 0) + plane_copies(ca, 0, 1)
+    for copy in ch_copies:
         copy.start()
     pending += rec_copies + zh_copies + ph_copies + ch_copies
 
-    @pl.loop(1, rows_x - 1)
-    def _(x):
-        copy_plane(x)
-
     for copy in rec_copies:
         copy.wait_recv()
-    table = jnp.concatenate([recg[d] for d in range(tiles)], axis=1)
+    if 2 * rec.shape[1] == LANES and tiles % 2 == 0:
+        table = jnp.concatenate([recg[d] + pltpu.roll(recg[d + 1], LANES // 2, 1)
+                                 for d in range(0, tiles, 2)], axis=1)
+    else:
+        table = jnp.concatenate([recg[d] for d in range(tiles)], axis=1)
     total = table.shape[1]
     start_x, len_x = table[0:1], table[1:2]
     start_y, len_y = table[2:3], table[3:4]
@@ -132,7 +147,7 @@
     def put_base(x, polymer):
         in_x = jnp.where(wrap(tile * rows_x + x - start_x) < len_x, 1.0, 0.0)
         values = polymer / (1.0 + BLOCKING * counted(in_z * in_x))
-        dst = pl.ds(pl.multiple_of((x + 1) * rows_z, rows_z), rows_z)
+        dst = pl.ds(pl.multiple_of((x + 1) * pitch, 8), rows_z)
         for j in range(halves):
             base[j, dst, :] = values[:, j * LANES:(j + 1) * LANES]
 
@@ -153,7 +168,7 @@
 
     def base_row(z):
         return jnp.stack([
-            base[j, pl.ds((1 + g * ROWS) * rows_z + z, ROWS, stride=rows_z), :]
+            base[j, pl.ds((1 + g * ROWS) * pitch + z, ROWS, stride=pitch), :]
             for g in range(groups) for j in range(halves)])
 
     first_base = base_row(0)
@@ -250,9 +265,9 @@
 
     def plane_x(c, x):
         for z in range(0, rows_z, 16):
-            under = pl.ds(pl.multiple_of(x * rows_z, rows_z) + z, 16)
-            here = pl.ds(pl.multiple_of((x + 1) * rows_z, rows_z) + z, 16)
-            over = pl.ds(pl.multiple_of((x + 2) * rows_z, rows_z) + z, 16)
+            under = pl.ds(pl.multiple_of(x * pitch, 8) + z, 16)
+            here = pl.ds(pl.multiple_of((x + 1) * pitch, 8) + z, 16)
+            over = pl.ds(pl.multiple_of((x + 2) * pitch, 8) + z, 16)
             b = [base[j, here, :] for j in range(halves)]
             b_next = next_y(b)
             face_xm = [0.5 * (base[j, under, :] + b[j]) for j in range(halves)]
@@ -271,7 +286,7 @@
 
     def strided(ref, z, pad):
         return jnp.stack([
-            ref[s, j, pl.ds((pad + g * ROWS) * rows_z + z, ROWS, stride=rows_z), :]
+            ref[s, j, pl.ds((pad + g * ROWS) * pitch + z, ROWS, stride=pitch), :]
             for s in range(species) for g in range(groups) for j in range(halves)])
 
     def put_strided(ref, z, pad, value):
@@ -279,7 +294,7 @@
         for s in range(species):
             for g in range(groups):
                 for j in range(halves):
-                    ref[s, j, pl.ds((pad + g * ROWS) * rows_z + z, ROWS, stride=rows_z), :] = value[n]
+                    ref[s, j, pl.ds((pad + g * ROWS) * pitch + z, ROWS, stride=pitch), :] = value[n]
                     n += 1
 
     def forward_rows(n, state):
@@ -331,12 +346,17 @@
 
     for step in range(STEPS):
         c_in = ca if step == 0 else cb
+
+        @pl.loop(1, rows_x - 1)
+        def _(x, c_in=c_in):
+            plane_x(c_in, x)
+
         for copy in ch_copies:
             copy.wait_recv()
 
-        @pl.loop(0, rows_x)
-        def _(x, c_in=c_in):
-            plane_x(c_in, x)
+        @pl.loop(0, 2)
+        def _(side, c_in=c_in):
+            plane_x(c_in, side * (rows_x - 1))
 
         lax.fori_loop(0, rows_z // unroll, forward_rows, jnp.zeros(shape, F32))
         first = lax.fori_loop(0, rows_z // unroll, backward_rows, jnp.zeros(shape, F32))
@@ -370,11 +390,17 @@
                             val[z] + spike_p[z] * before + spike_q[z] * after)
             return carry
 
-        lax.fori_loop(0, rows_z // unroll, finish_rows, 0)
+        half = rows_z // unroll // 2
+        sent = []
+        for part in range(2):
+            lax.fori_loop(part * half, (part + 1) * half, finish_rows, 0)
+            if step + 1 < STEPS:
+                copies = plane_copies(cb, step + 1, part)
+                for copy in copies:
+                    copy.start()
+                sent += copies
         if step + 1 < STEPS:
-            ch_copies = plane_copies(cb, step + 1)
-            for copy in ch_copies:
-                copy.start()
+            ch_copies = sent
             pending += ch_copies
         if step == 0:
             for copy in pending:
@@ -388,7 +414,7 @@
 
     @pl.loop(0, rows_x)
     def _(x):
-        src = pl.ds(pl.multiple_of((x + 1) * rows_z, rows_z), rows_z)
+        src = pl.ds(pl.multiple_of((x + 1) * pitch, 8), rows_z)
         for s in range(species):
             for j in range(halves):
                 out[s, x, :, j * LANES:(j + 1) * LANES] = ca[s, j, src, :]
@@ -404,19 +430,22 @@
     halves = width_y // LANES
     chunks = species * (rows_x // ROWS) * halves
     count = plates.shape[0]
-    records = jnp.pad(plates.T, ((0, 8 - plates.shape[1]), (0, -count % LANES)))
+    padded = (8, count + -count % LANES)
+    records = plates.T
     line = pltpu.VMEM((rows_z, chunks, ROWS, LANES), F32)
     dma = pltpu.SemaphoreType.DMA
-    extended = (halves, (rows_x + 2) * rows_z, LANES)
+    extended = (halves, (rows_x + 2) * (rows_z + PAD), LANES)
     scratch = [
-        pltpu.VMEM((tiles,) + records.shape, jnp.int32),
+        pltpu.VMEM(padded, jnp.int32),
+        pltpu.VMEM((tiles,) + padded, jnp.int32),
+        pltpu.VMEM(polymer.shape, F32),
         pltpu.VMEM((2, rows_x, width_y), F32),
         pltpu.VMEM((2, rows_x, width_y), F32),
         pltpu.VMEM((2, rows_z, width_y), F32),
         pltpu.VMEM(extended, F32),
         pltpu.VMEM((species,) + extended, F32),
         pltpu.VMEM((species,) + extended, F32),
-        pltpu.VMEM((species, halves, rows_x * rows_z, LANES), F32),
+        pltpu.VMEM((species, halves, rows_x * (rows_z + PAD), LANES), F32),
         line, line, line, line, line, line,
         pltpu.VMEM((chunks, 4, ROWS, LANES), F32),
         pltpu.VMEM((layers, 4, ROWS, LANES), F32),
@@ -426,18 +455,20 @@
         pltpu.VMEM((STEPS, layers, 2, ROWS, LANES), F32),
         pltpu.VMEM((STEPS, chunks, 2, ROWS, LANES), F32),
         dma((tiles,)), dma((tiles,)), dma((2,)), dma((2,)), dma((2,)), dma((2,)),
-        dma((STEPS, 2)), dma((STEPS, 2)), dma((layers,)), dma((layers,)),
+        dma((STEPS, 2, 2)), dma((STEPS, 2, 2)), dma((layers,)), dma((layers,)),
         dma((STEPS, layers)), dma((STEPS, layers)), dma((STEPS, layers)), dma((STEPS, layers)),
+        dma, dma,
     ]
     vmem = pl.BlockSpec(memory_space=pltpu.VMEM)
+    hbm = pl.BlockSpec(memory_space=pltpu.HBM)
     return pl.pallas_call(
         functools.partial(kernel, tiles, layers),
         out_shape=jax.ShapeDtypeStruct(concentration.shape, F32),
-        in_specs=[vmem, vmem, vmem],
+        in_specs=[hbm, hbm, vmem],
         out_specs=vmem,
         scratch_shapes=scratch,
         compiler_params=pltpu.CompilerParams(
-            collective_id=0, has_side_effects=True, vmem_limit_bytes=48 * 2**20),
+            collective_id=0, has_side_effects=True, vmem_limit_bytes=62 * 2**20),
     )(concentration, polymer, records)
 
 

time: 60.9 us -> 50.6 us (0.83)
  Pallas kernels: 55.9 us -> 47.3 us
  local copies, waits for them, and re-layouts: 4.83 us -> 3.13 us
    pallas_call x1, Pallas kernels: 55.9 us -> 47.3 us  [on_device(): pl.pallas_call(functools.partial(kernel, tiles, layers), out_shape=jax.Sh...]
    unnamed x5 -> x1, local copies, waits for them, and re-layouts: 4.14 us -> 3.13 us
    pad x1 -> x0, local copies, waits for them, and re-layouts: 0.69 us -> none  [on_device(): records = jnp.pad(plates.T, ((0, 8 - plates.shape[1]), (0, -count % LANES)))]
where the time goes in v1:
time: 50.6 us; the launch traced here: 50.5 us
  Pallas kernels  47.3 us (93%)
  local copies, waits for them, and re-layouts  3.13 us (6%)
    pallas_call x1, Pallas kernels, on_device(): pl.pallas_call(functools.partial(kernel, tiles, layers), out_shape=jax.Sh...  47.3 us
    unnamed x1, local copies, waits for them, and re-layouts  3.13 us

profile of v1, /device:TPU:0, one launch (start us, length us, event | category | flops | bytes accessed | tf_op | source)
XLA Modules:
  0.0 50.5 jit_solution(18183601206209769250)
XLA Ops:
  0.0 47.3 %shard_map.37 = f32[2,16,64,256]{3,2,1,0:T(8,128)} custom-call(f32[2,16,64,256]{3,2,1,0:T(8,128)} %conc.1, f32[16,64,256]{2,1,0:T(8,128)} %poly_in.1, s32[6,64]{1,0:T(8,128)} %bitcast.1), custom_call_target="tpu_custom_call" | custom-call | tf_op jit(solution)/shard_map/pallas_call | solution.py:464
  47.3 3.1 %copy.5 = f32[2,16,64,256]{3,2,1,0:T(8,128)} copy(f32[2,16,64,256]{3,2,1,0:T(8,128)} %shard_map.37) | data formatting | bytes 4194304

commit v2 on v1

--- a/solution.py
+++ b/solution.py
@@ -45,6 +45,12 @@
         else:
             pl.when(cond)(fn)
 
+    def when_owner(owner, lo, hi, fn):
+        if lo == 0 and hi == chunks:
+            when(owner < chunks, fn)
+        else:
+            pl.when((owner >= lo) & (owner < hi))(fn)
+
     def remote(src, dst, send, recv, where):
         return pltpu.make_async_remote_copy(
             src_ref=src, dst_ref=dst, send_sem=send, recv_sem=recv,
@@ -89,16 +95,14 @@
     ]
 
     def plane_copies(c, step, part):
-        span = rows_z // 2
-        low_row = part * span
-        last = pl.ds(rows_x * pitch + low_row, span)
-        first = pl.ds(pitch + low_row, span)
-        over = pl.ds((rows_x + 1) * pitch + low_row, span)
-        under = pl.ds(low_row, span)
+        last = pl.ds(rows_x * pitch, rows_z)
+        first = pl.ds(pitch, rows_z)
+        over = pl.ds((rows_x + 1) * pitch, rows_z)
+        under = pl.ds(0, rows_z)
         return [
-            remote(c.at[:, :, last, :], c.at[:, :, under, :], ch_s.at[step, part, 0],
+            remote(c.at[part, :, last, :], c.at[part, :, under, :], ch_s.at[step, part, 0],
                    ch_r.at[step, part, 0], (tile_at(1), layer)),
-            remote(c.at[:, :, first, :], c.at[:, :, over, :], ch_s.at[step, part, 1],
+            remote(c.at[part, :, first, :], c.at[part, :, over, :], ch_s.at[step, part, 1],
                    ch_r.at[step, part, 1], (tile_at(-1), layer)),
         ]
 
@@ -224,15 +228,15 @@
         return owner, remote(src.at[owner if every else lax.rem(owner, chunks)], dst.at[layer],
                              send, recv, (tile, owner))
 
-    def send_owned(src, dst, send, recv):
+    def send_owned(src, dst, send, recv, lo=0, hi=chunks):
         for d in range(1, layers):
             owner, copy = to_owner(src, dst, send(d), recv(d), d)
-            when(owner < chunks, copy.start)
+            when_owner(owner, lo, hi, copy.start)
 
         def keep():
             dst[layer] = src[layer if every else lax.rem(layer, chunks)]
 
-        when(layer < chunks, keep)
+        when_owner(layer, lo, hi, keep)
 
     def wait_owned(src, dst, send, recv):
         for d in range(1, layers):
@@ -263,7 +267,7 @@
         turned = [pltpu.roll(v, 1, 1) for v in parts]
         return [jnp.where(lane == 0, turned[j - 1], turned[j]) for j in range(halves)]
 
-    def plane_x(c, x):
+    def plane_x(c, x, s):
         for z in range(0, rows_z, 16):
             under = pl.ds(pl.multiple_of(x * pitch, 8) + z, 16)
             here = pl.ds(pl.multiple_of((x + 1) * pitch, 8) + z, 16)
@@ -273,42 +277,41 @@
             face_xm = [0.5 * (base[j, under, :] + b[j]) for j in range(halves)]
             face_xp = [0.5 * (b[j] + base[j, over, :]) for j in range(halves)]
             face_y = [0.5 * (b[j] + b_next[j]) for j in range(halves)]
-            for s in range(species):
-                v = [c[s, j, here, :] for j in range(halves)]
-                v_next = next_y(v)
-                flux = [face_y[j] * (v_next[j] - v[j]) for j in range(halves)]
-                back = prior_y(flux)
-                for j in range(halves):
-                    along = (face_xp[j] * (c[s, j, over, :] - v[j])
-                             - face_xm[j] * (v[j] - c[s, j, under, :]))
-                    rhs[s, j, under, :] = v[j] + (PLANE_RATE * RATIOS[s]) * (
-                        along + (flux[j] - back[j]))
-
-    def strided(ref, z, pad):
+            v = [c[s, j, here, :] for j in range(halves)]
+            v_next = next_y(v)
+            flux = [face_y[j] * (v_next[j] - v[j]) for j in range(halves)]
+            back = prior_y(flux)
+            for j in range(halves):
+                along = (face_xp[j] * (c[s, j, over, :] - v[j])
+                         - face_xm[j] * (v[j] - c[s, j, under, :]))
+                rhs[s, j, under, :] = v[j] + (PLANE_RATE * RATIOS[s]) * (
+                    along + (flux[j] - back[j]))
+
+    def strided(ref, z, s):
         return jnp.stack([
-            ref[s, j, pl.ds((pad + g * ROWS) * pitch + z, ROWS, stride=pitch), :]
-            for s in range(species) for g in range(groups) for j in range(halves)])
-
-    def put_strided(ref, z, pad, value):
-        n = 0
-        for s in range(species):
-            for g in range(groups):
-                for j in range(halves):
-                    ref[s, j, pl.ds((pad + g * ROWS) * pitch + z, ROWS, stride=pitch), :] = value[n]
-                    n += 1
-
-    def forward_rows(n, state):
+            ref[s, j, pl.ds(g * ROWS * pitch + z, ROWS, stride=pitch), :]
+            for g in range(groups) for j in range(halves)])
+
+    def put_strided(ref, z, s, value):
+        for g in range(groups):
+            for j in range(halves):
+                ref[s, j, pl.ds((1 + g * ROWS) * pitch + z, ROWS, stride=pitch), :] = (
+                    value[g * halves + j])
+
+    def forward_rows(s, n, state):
+        own = slice(s * per, (s + 1) * per)
         for m in range(unroll):
             z = n * unroll + m
-            state = strided(rhs, z, 0) * inv[z] - low[z] * state
-            val[z] = state
+            state = strided(rhs, z, s) * inv[z, own] - low[z, own] * state
+            val[z, own] = state
         return state
 
-    def backward_rows(n, v):
+    def backward_rows(s, n, v):
+        own = slice(s * per, (s + 1) * per)
         for m in range(unroll):
             z = rows_z - 1 - (n * unroll + m)
-            v = val[z] - fac[z] * v
-            val[z] = v
+            v = val[z, own] - fac[z, own] * v
+            val[z, own] = v
         return v
 
     def reduce_matrix():
@@ -346,27 +349,27 @@
 
     for step in range(STEPS):
         c_in = ca if step == 0 else cb
-
-        @pl.loop(1, rows_x - 1)
-        def _(x, c_in=c_in):
-            plane_x(c_in, x)
-
-        for copy in ch_copies:
-            copy.wait_recv()
-
-        @pl.loop(0, 2)
-        def _(side, c_in=c_in):
-            plane_x(c_in, side * (rows_x - 1))
-
-        lax.fori_loop(0, rows_z // unroll, forward_rows, jnp.zeros(shape, F32))
-        first = lax.fori_loop(0, rows_z // unroll, backward_rows, jnp.zeros(shape, F32))
-        last = val[rows_z - 1]
-        for c in range(chunks):
-            ends_out[step, c, 0] = first[c]
-            ends_out[step, c, 1] = last[c]
         ends_args = (ends_out.at[step], ends_in.at[step],
                      lambda d, step=step: en_s.at[step, d], lambda d, step=step: en_r.at[step, d])
-        send_owned(*ends_args)
+        for s in range(species):
+            @pl.loop(1, rows_x - 1)
+            def _(x, c_in=c_in, s=s):
+                plane_x(c_in, x, s)
+
+            for copy in ch_copies[2 * s:2 * s + 2]:
+                copy.wait_recv()
+
+            @pl.loop(0, 2)
+            def _(side, c_in=c_in, s=s):
+                plane_x(c_in, side * (rows_x - 1), s)
+
+            zero = jnp.zeros((per, ROWS, LANES), F32)
+            lax.fori_loop(0, rows_z // unroll, functools.partial(forward_rows, s), zero)
+            first = lax.fori_loop(0, rows_z // unroll, functools.partial(backward_rows, s), zero)
+            for c in range(per):
+                ends_out[step, s * per + c, 0] = first[c]
+                ends_out[step, s * per + c, 1] = val[rows_z - 1, s * per + c]
+            send_owned(*ends_args, s * per, (s + 1) * per)
         if step == 0:
             when(layer < chunks, reduce_matrix)
         wait_owned(*ends_args)
@@ -378,24 +381,24 @@
             sides[step, layer if every else lax.rem(layer, chunks)] = reply[step, layer]
 
         when(layer < chunks, answer)
-        for d in range(1, layers):
-            when(layer_at(-d) < chunks, reply_copy(step, d).wait_recv)
-        before = sides[step, :, 0]
-        after = sides[step, :, 1]
-
-        def finish_rows(n, carry):
-            for m in range(unroll):
-                z = n * unroll + m
-                put_strided(cb if step + 1 < STEPS else ca, z, 1,
-                            val[z] + spike_p[z] * before + spike_q[z] * after)
-            return carry
-
-        half = rows_z // unroll // 2
         sent = []
-        for part in range(2):
-            lax.fori_loop(part * half, (part + 1) * half, finish_rows, 0)
+        for s in range(species):
+            own = slice(s * per, (s + 1) * per)
+            for d in range(1, layers):
+                when_owner(layer_at(-d), s * per, (s + 1) * per, reply_copy(step, d).wait_recv)
+            before = sides[step, own, 0]
+            after = sides[step, own, 1]
+
+            def finish_rows(n, carry, s=s, own=own, before=before, after=after):
+                for m in range(unroll):
+                    z = n * unroll + m
+                    put_strided(cb if step + 1 < STEPS else ca, z, s,
+                                val[z, own] + spike_p[z, own] * before + spike_q[z, own] * after)
+                return carry
+
+            lax.fori_loop(0, rows_z // unroll, finish_rows, 0)
             if step + 1 < STEPS:
-                copies = plane_copies(cb, step + 1, part)
+                copies = plane_copies(cb, step + 1, s)
                 for copy in copies:
                     copy.start()
                 sent += copies

time: 50.6 us -> 51.8 us (1.024)
  Pallas kernels: 47.3 us -> 48.5 us
    pallas_call x1, Pallas kernels: 47.3 us -> 48.5 us  [on_device(): pl.pallas_call(functools.partial(kernel, tiles, layers), out_shape=jax.Sh...]
where the time goes in v2:
time: 51.8 us; the launch traced here: 51.6 us
  Pallas kernels  48.5 us (94%)
  local copies, waits for them, and re-layouts  3.13 us (6%)
    pallas_call x1, Pallas kernels, on_device(): pl.pallas_call(functools.partial(kernel, tiles, layers), out_shape=jax.Sh...  48.5 us
    unnamed x1, local copies, waits for them, and re-layouts  3.13 us

profile of v2, /device:TPU:0, one launch (start us, length us, event | category | flops | bytes accessed | tf_op | source)
XLA Modules:
  0.0 51.6 jit_solution(8714821982602790412)
XLA Ops:
  0.0 48.5 %shard_map.37 = f32[2,16,64,256]{3,2,1,0:T(8,128)} custom-call(f32[2,16,64,256]{3,2,1,0:T(8,128)} %conc.1, f32[16,64,256]{2,1,0:T(8,128)} %poly_in.1, s32[6,64]{1,0:T(8,128)} %bitcast.1), custom_call_target="tpu_custom_call" | custom-call | tf_op jit(solution)/shard_map/pallas_call | solution.py:467
  48.5 3.1 %copy.5 = f32[2,16,64,256]{3,2,1,0:T(8,128)} copy(f32[2,16,64,256]{3,2,1,0:T(8,128)} %shard_map.37) | data formatting | bytes 4194304
